TPU v7x, 128 devices: a whole 4x4x4 slice. The times are simulated.
128 devices in a mesh: dp: 16 (over z, y_lo, core), mp: 8 (over x, y_hi).
Axes of the slice: x: 4, y: 4 (y_hi: 2, y_lo: 2; y = y_hi * 2 + y_lo), z: 4, core: 2. Of those that a mesh axis runs over, the one named last changes fastest.
Arguments:
- gradients: bfloat16 [16, 2560, 16384], P('dp', 'mp'), may hold values from -2.5 to 2.5
- left_basis: bfloat16 [2560, 2560], P('dp', 'mp'), may hold values from -0.125 to 0.125
- right_basis: bfloat16 [16, 1024, 1024], P('dp'), may hold values from -0.1875 to 0.1875
- first_moment: float32 [2560, 16384], P('mp', 'dp'), may hold values from -3 to 3
- second_moment: float32 [2560, 16384], P('mp', 'dp'), may hold values from 0.004 to 0.1
- left_stats: float32 [2560, 2560], P('dp', 'mp'), may hold values from -6 to 6
- right_stats: float32 [16, 1024, 1024], P('dp', 'mp'), may hold values from -6 to 6
Outputs:
- update: bfloat16 [2560, 16384], P('mp', 'dp')
- new_first: float32 [2560, 16384], P('mp', 'dp')
- new_second: float32 [2560, 16384], P('mp', 'dp')
- new_left: float32 [2560, 2560], P('dp', 'mp')
- new_right: float32 [16, 1024, 1024], P('dp', 'mp')
All inputs are finite; a program needn't handle non-finite values.
Results may differ from a plain program's by a relative error of at most 0.028.
Values may be sent and summed in bfloat16 or wider, within the bound.
A program may use at most 128 MiB of HBM per device.

v0:
```python
import jax
import jax.numpy as jnp
from jax import lax
from jax.sharding import PartitionSpec as P

beta_first = 0.9
beta_second = 0.95
beta_stats = 0.95
epsilon = 1e-08


def on_device(
    gradients, left_basis, right_basis, first_moment, second_moment, left_stats, right_stats
):
    summed = lax.psum_scatter(
        gradients[0].astype(jnp.float32).astype(jnp.bfloat16), "dp", scatter_dimension=1, tiled=True
    )
    columns = lax.all_gather(summed, "mp", axis=0, tiled=True)
    column_panel = lax.all_gather(left_basis, "dp", axis=0, tiled=True)
    rotated = lax.dot_general(
        column_panel, columns, (((0,), (0,)), ((), ())), preferred_element_type=jnp.float32
    ).astype(jnp.bfloat16)
    block_basis = right_basis[0]
    turned = jnp.dot(rotated, block_basis, preferred_element_type=jnp.float32)
    new_first = beta_first * first_moment + (1.0 - beta_first) * turned
    new_second = beta_second * second_moment + (1.0 - beta_second) * turned * turned
    scaled = (new_first / (jnp.sqrt(new_second) + epsilon)).astype(jnp.bfloat16)
    back = lax.dot_general(
        scaled, block_basis, (((1,), (1,)), ((), ())), preferred_element_type=jnp.float32
    ).astype(jnp.bfloat16)
    assembled = lax.psum_scatter(
        jnp.dot(column_panel, back, preferred_element_type=jnp.float32).astype(jnp.bfloat16),
        "mp",
        scatter_dimension=0,
        tiled=True,
    )
    outer_left = lax.psum_scatter(
        lax.dot_general(
            columns, summed, (((1,), (1,)), ((), ())), preferred_element_type=jnp.float32
        ).astype(jnp.bfloat16),
        "dp",
        scatter_dimension=0,
        tiled=True,
    ).astype(jnp.float32)
    new_left = beta_stats * left_stats + (1.0 - beta_stats) * outer_left
    share_rows = right_stats.shape[1]
    offset = lax.axis_index("mp") * share_rows
    column_slice = lax.dynamic_slice_in_dim(columns, offset, share_rows, 1)
    outer_right = lax.dot_general(
        column_slice, columns, (((0,), (0,)), ((), ())), preferred_element_type=jnp.float32
    )
    new_right = (beta_stats * right_stats[0] + (1.0 - beta_stats) * outer_right)[None]
    return (assembled, new_first, new_second, new_left, new_right)


def solution(mesh):
    return jax.shard_map(
        on_device,
        mesh=mesh,
        in_specs=(
            P("dp", "mp", None),
            P("dp", "mp"),
            P("dp", None, None),
            P("mp", "dp"),
            P("mp", "dp"),
            P("dp", "mp"),
            P("dp", "mp", None),
        ),
        out_specs=(P("mp", "dp"), P("mp", "dp"), P("mp", "dp"), P("dp", "mp"), P("dp", "mp", None)),
        check_vma=False,
    )
```

profile of v0, /device:TPU:0, one launch (start us, length us, event | category | flops | bytes accessed | tf_op | source)
XLA Modules:
  0.0 414.6 jit_solution(15690689691286418319)
XLA Ops:
  7.2 0.0 copy-start
  7.2 0.0 reduce-scatter.6.cloned.1.call-start
  7.2 0.7 reduce-scatter.6.cloned.1.call-update
  7.9 0.0 all-gather.5.cloned.1.call-start
  8.0 124.1 %reduce-scatter.6.cloned.1.call-done = bf16[320,1024]{1,0:T(8,128)(2,1)} async-done(((bf16[320,16384]{1,0:T(8,128)(2,1)}), bf16[320,1024]{1,0:T(8,128)(2,1)}) %reduce-scatter.6.cloned.1.call-update) | async-done | bytes 655376 | tf_op jit(solution)/shard_map/reduce_scatter | solution.py:15
  132.1 0.0 all-gather.5.cloned.1.call-update
  132.1 0.0 all-gather.3.cloned.1.call-start
  132.1 0.7 all-gather.3.cloned.1.call-update
  132.8 0.0 reduce-scatter.8.cloned.1.call-start
  132.9 80.3 %all-gather.5.cloned.1.call-done = bf16[2560,1024]{1,0:T(8,128)(2,1)} async-done(((bf16[320,1024]{1,0:T(8,128)(2,1)}), bf16[2560,1024]{1,0:T(8,128)(2,1)}) %all-gather.5.cloned.1.call-update) | async-done | bytes 5242896 | tf_op jit(solution)/shard_map/all_gather | solution.py:18
  213.2 6.8 %convolution_convert_fusion.1 = bf16[2560,320]{1,0:T(8,128)(2,1)} fusion(bf16[2560,1024]{1,0:T(8,128)(2,1)} %all-gather.5.cloned.1.call-done, bf16[320,1024]{1,0:T(8,128)(2,1)} %reduce-scatter.6.cloned.1.call-done), kind=kOutput, calls=%fused_computation.2 | convolution fusion | flops 1678540800 | bytes 7536640 | tf_op jit(solution)/shard_map/dot_general | solution.py:38
  220.0 0.0 copy-start.3
  220.0 0.0 reduce-scatter.8.cloned.1.call-update
  220.0 0.0 reduce-scatter.10.cloned.1.call-start
  220.1 27.0 %all-gather.3.cloned.1.call-done = bf16[2560,320]{1,0:T(8,128)(2,1)} async-done(((bf16[160,320]{1,0:T(8,128)(2,1)}), bf16[2560,320]{1,0:T(8,128)(2,1)}) %all-gather.3.cloned.1.call-update) | async-done | bytes 1638416 | tf_op jit(solution)/shard_map/all_gather | solution.py:19
  247.1 0.0 copy-done
  247.1 0.0 copy-done.3
  247.1 7.7 %fusion.8 = (f32[320,1024]{1,0:T(8,128)}, f32[320,1024]{1,0:T(8,128)}) fusion(f32[320,1024]{1,0:T(8,128)S(1)} %copy-done.3, f32[320,1024]{1,0:T(8,128)} %param.10, bf16[1,1024,1024]{2,1,0:T(8,128)(2,1)S(1)} %copy-done, bf16[2560,320]{1,0:T(8,128)(2,1)} %all-gather.3.cloned.1.call-done, bf16[2560,1024]{1,0:T(8,128)(2,1)} %all-gather.5.cloned.1.call-done), kind=kOutput, calls=%fused_computation.10 | convolution fusion | flops 2351431680 | bytes 14221312 | tf_op jit(solution)/shard_map/dot_general | solution.py:24
  254.8 8.5 %fusion = bf16[2560,1024]{0,1:T(8,128)(2,1)} fusion(bf16[2560,320]{1,0:T(8,128)(2,1)} %all-gather.3.cloned.1.call-done, bf16[1,1024,1024]{2,1,0:T(8,128)(2,1)S(1)} %copy-done, f32[320,1024]{1,0:T(8,128)} %get-tuple-element.16, f32[320,1024]{1,0:T(8,128)} %get-tuple-element.15), kind=kOutput, calls=%fused_computation.1 | convolution fusion | flops 2352742400 | bytes 11599872 | tf_op jit(solution)/shard_map/dot_general | solution.py:32
  263.3 8.0 %copy.14 = bf16[2560,1024]{1,0:T(8,128)(2,1)} copy(bf16[2560,1024]{0,1:T(8,128)(2,1)} %fusion) | data formatting | bytes 10485760
  271.3 0.0 copy-start.1
  271.3 0.0 reduce-scatter.10.cloned.1.call-update
  271.3 1.0 copy-done.1
  272.3 0.0 copy-start.2
  272.3 4.4 %fusion.10 = f32[1,128,1024]{2,1,0:T(8,128)} fusion(bf16[2560,1024]{1,0:T(8,128)(2,1)} %all-gather.5.cloned.1.call-done, s32[]{:T(128)S(6)} %select_n.3, f32[1,128,1024]{2,1,0:T(8,128)S(1)} %copy-done.1), kind=kOutput, calls=%fused_computation.15 | convolution fusion | flops 671481856 | bytes 6946820 | tf_op jit(solution)/shard_map/dot_general | solution.py:49
  276.7 36.4 %reduce-scatter.8.cloned.1.call-done = bf16[160,320]{1,0:T(8,128)(2,1)} async-done(((bf16[2560,320]{1,0:T(8,128)(2,1)}), bf16[160,320]{1,0:T(8,128)(2,1)}) %reduce-scatter.8.cloned.1.call-update) | async-done | bytes 102416 | tf_op jit(solution)/shard_map/reduce_scatter | solution.py:37
  313.1 0.0 copy-done.2
  313.1 1.6 multiply_add_fusion.1
  314.8 93.3 %reduce-scatter.10.cloned.1.call-done = bf16[320,1024]{1,0:T(8,128)(2,1)} async-done(((bf16[2560,1024]{1,0:T(8,128)(2,1)}), bf16[320,1024]{1,0:T(8,128)(2,1)}) %reduce-scatter.10.cloned.1.call-update) | async-done | bytes 655376
Async XLA Ops:
  7.2 239.9 %copy-start = (bf16[1,1024,1024]{2,1,0:T(8,128)(2,1)S(1)}, bf16[1,1024,1024]{2,1,0:T(8,128)(2,1)}, u32[]{:S(2)}) copy-start(bf16[1,1024,1024]{2,1,0:T(8,128)(2,1)} %param.9) | copy-start | bytes 6291460
  7.2 124.9 %reduce-scatter.6.cloned.1.call-start = ((), (), s32[]{:S(2)}) async-start(), calls=%async_computation.4 | async-start | bytes 11141120 | tf_op jit(solution)/shard_map/reduce_scatter | solution.py:15
  7.9 205.3 %all-gather.5.cloned.1.call-start = ((), (), s32[]{:S(2)}) async-start(), calls=%async_computation.5 | async-start | bytes 5898240 | tf_op jit(solution)/shard_map/all_gather | solution.py:18
  132.1 115.0 %all-gather.3.cloned.1.call-start = ((), (), s32[]{:S(2)}) async-start(), calls=%async_computation.3 | async-start | bytes 2088960 | tf_op jit(solution)/shard_map/all_gather | solution.py:19
  132.8 180.3 %reduce-scatter.8.cloned.1.call-start = ((), (), s32[]{:S(2)}) async-start(), calls=%async_computation.6 | async-start | bytes 2088960 | tf_op jit(solution)/shard_map/reduce_scatter | solution.py:37
  220.0 27.1 %copy-start.3 = (f32[320,1024]{1,0:T(8,128)S(1)}, f32[320,1024]{1,0:T(8,128)}, u32[]{:S(2)}) copy-start(f32[320,1024]{1,0:T(8,128)} %param.11) | copy-start | bytes 3932164
  220.0 188.0 %reduce-scatter.10.cloned.1.call-start = ((), (), s32[]{:S(2)}) async-start(), calls=%async_computation.7 | async-start | bytes 5898240
  271.3 1.0 copy-start.1
  272.3 40.8 %copy-start.2 = (f32[160,320]{1,0:T(8,128)S(1)}, f32[160,320]{1,0:T(8,128)}, u32[]{:S(2)}) copy-start(f32[160,320]{1,0:T(8,128)} %param.12) | copy-start | bytes 614404
Sparse Core Ops, SparseCore 0:
  10.4 121.6 reduce-scatter.5
  134.4 78.7 all-gather.4
  214.9 32.1 all-gather.2
  249.4 63.7 reduce-scatter.7
  318.0 90.0 reduce-scatter.9
where the time goes:
time: 415 us
  waiting for transfers between devices  363 us (87%)
  matrix products  27.4 us (7%)
  between operations  13.8 us (3%)
  local copies, waits for them, and re-layouts  8.99 us (2%)
    reduce_scatter x1, waiting for transfers between devices, on_device(): lax.psum_scatter(gradients[0].astype(jnp.float32).astype(jnp.bfloat16), '...  124 us
    unnamed x6, waiting for transfers between devices  94.7 us
    all_gather x1, waiting for transfers between devices, on_device(): columns = lax.all_gather(summed, 'mp', axis=0, tiled=True)  80.3 us
    reduce_scatter x1, waiting for transfers between devices, on_device(): lax.psum_scatter(lax.dot_general(columns, summed, (((1,), (1,)), ((), ())...  36.4 us
    all_gather x1, waiting for transfers between devices, on_device(): column_panel = lax.all_gather(left_basis, 'dp', axis=0, tiled=True)  27 us
    unnamed x9, local copies, waits for them, and re-layouts  8.99 us
    dot_general x1, matrix products, on_device(): jnp.dot(column_panel, back, preferred_element_type=jnp.float32)  8.5 us
  transfers between devices with their start and end apart: 5, of which 5 were waited for; matrix products, arithmetic and copies ran while one was open for 9% of the time, Pallas kernels for 0%

commit v1 on v0

--- a/solution.py
+++ b/solution.py
@@ -1,22 +1,291 @@
+import functools
+
 import jax
 import jax.numpy as jnp
 from jax import lax
+from jax.experimental import pallas as pl
+from jax.experimental.pallas import tpu as pltpu
 from jax.sharding import PartitionSpec as P
 
+MESH = pl.DeviceIdType.MESH
 beta_first = 0.9
 beta_second = 0.95
 beta_stats = 0.95
 epsilon = 1e-08
 
+F32 = jnp.float32
+BF16 = jnp.bfloat16
+
+
+def local_copy(src, dst, sem):
+    return pltpu.make_async_copy(src, dst, sem)
+
+
+def remote_copy(src, dst, send, recv, **device):
+    return pltpu.make_async_remote_copy(
+        src_ref=src,
+        dst_ref=dst,
+        send_sem=send,
+        recv_sem=recv,
+        device_id=device,
+        device_id_type=MESH,
+    )
+
+
+def arrived(ref, sem):
+    pltpu.make_async_copy(ref, ref, sem).wait()
+
+
+def gather_kernel(
+    chunks,
+    grads, left,
+    cols_out, panel_out,
+    own, swap, ring, pair, cols, panel,
+    own_sem, swap_send, swap_recv, ring_send, ring_recv, pair_send, pair_recv,
+    gather_send, gather_recv, panel_send, panel_recv, out_sem,
+):
+    dp = lax.axis_index("dp")
+    mp = lax.axis_index("mp")
+    z, yl, c = dp // 4, (dp // 2) % 2, dp % 2
+    x, yh = mp // 2, mp % 2
+    zn, zp, zo = (z + 1) % 4, (z + 3) % 4, (z + 2) % 4
+    xn, xp, xo = (x + 1) % 4, (x + 3) % 4, (x + 2) % 4
+    core_peer = {"dp": z * 4 + yl * 2 + (1 - c)}
+    y_peer = {"dp": z * 4 + (1 - yl) * 2 + c}
+    z_next = {"dp": zn * 4 + yl * 2 + c}
+    z_prev = {"dp": zp * 4 + yl * 2 + c}
+    h_peer = {"mp": x * 2 + (1 - yh)}
+    x_next = {"mp": xn * 2 + yh}
+    x_prev = {"mp": xp * 2 + yh}
+    partners = (core_peer, y_peer, z_next, z_prev, h_peer, x_next, x_prev)
+
+    rows, width = own.shape[2], own.shape[3]
+    block = width * chunks
+    half = rows // 2
+
+    def columns(owner, k):
+        return pl.ds(pl.multiple_of(owner * block + k * width, 128), width)
+
+    local_copy(left, panel.at[c, z * 2 + yl], out_sem.at[0]).start()
+    for k in range(chunks):
+        for j in range(8):
+            local_copy(
+                grads.at[0, :, columns(j * 2 + c, k)], own.at[k, j], own_sem.at[k]
+            ).start()
+
+    barrier = pltpu.get_barrier_semaphore()
+    for p in partners:
+        pl.semaphore_signal(barrier, inc=1, device_id=p, device_id_type=MESH)
+    pl.semaphore_wait(barrier, len(partners))
+
+    for k in range(chunks):
+        for j in range(8):
+            remote_copy(
+                grads.at[0, :, columns(j * 2 + 1 - c, k)], swap.at[k, j],
+                swap_send.at[k], swap_recv.at[k], **core_peer,
+            ).start()
+
+    me = z * 2 + yl
+    arrived(panel.at[0, 0], out_sem.at[0])
+
+    def panel_copy(i, slot, n, **device):
+        return remote_copy(
+            panel.at[c, slot], panel.at[c, slot], panel_send.at[n], panel_recv.at[n], **device
+        )
+
+    panel_copy(c, me, 0, **y_peer).start()
+    panel_copy(c, me, 1, **z_next).start()
+    panel_copy(c, me, 2, **z_prev).start()
+
+    def panel_forward():
+        one = panel.at[0, 0]
+        arrived(one, panel_recv.at[0])
+        other = z * 2 + 1 - yl
+        panel_copy(c, other, 3, **z_next).start()
+        panel_copy(c, other, 4, **z_prev).start()
+        arrived(one, panel_recv.at[1])
+        panel_copy(c, zp * 2 + yl, 5, **z_next).start()
+        arrived(one, panel_recv.at[2])
+        arrived(one, panel_recv.at[4])
+        panel_copy(c, zn * 2 + 1 - yl, 6, **z_prev).start()
+
+    def panel_share():
+        one = panel.at[0, 0]
+        for n in (3, 5, 6):
+            arrived(one, panel_recv.at[n])
+        remote_copy(
+            panel.at[c], panel.at[c], panel_send.at[7], panel_recv.at[7], **core_peer
+        ).start()
+
+    def ring_copy(k, j, slot, **device):
+        remote_copy(
+            own.at[k, j], ring.at[k, slot], ring_send.at[k, slot], ring_recv.at[k, slot], **device
+        ).start()
+
+    def e1(k):
+        arrived(own.at[k], own_sem.at[k])
+        arrived(swap.at[k], swap_recv.at[k])
+
+        def add(j):
+            own[k, j] = (own[k, j].astype(F32) + swap[k, j].astype(F32)).astype(BF16)
+
+        add(zo * 2)
+        ring_copy(k, zo * 2, 0, **z_next)
+        add(zo * 2 + 1)
+        ring_copy(k, zo * 2 + 1, 1, **z_prev)
+        add(zn * 2 + 1)
+        ring_copy(k, zn * 2 + 1, 3, **z_next)
+        add(zp * 2)
+        ring_copy(k, zp * 2, 4, **z_prev)
+        add(zn * 2)
+        add(zp * 2 + 1)
+        add(z * 2)
+        add(z * 2 + 1)
+
+    def e2(k):
+        arrived(ring.at[k, 0], ring_recv.at[k, 0])
+        j = zn * 2
+        own[k, j] = (own[k, j].astype(F32) + ring[k, 0].astype(F32)).astype(BF16)
+        ring_copy(k, j, 2, **z_next)
+        arrived(ring.at[k, 1], ring_recv.at[k, 1])
+        i = zp * 2 + 1
+        own[k, i] = (own[k, i].astype(F32) + ring[k, 1].astype(F32)).astype(BF16)
+        ring_copy(k, i, 5, **z_prev)
+
+    def e3(k):
+        for slot in (3, 4, 2, 5):
+            arrived(ring.at[k, slot], ring_recv.at[k, slot])
+        j = z * 2 + 1 - yl
+        own[k, j] = (
+            own[k, j].astype(F32)
+            + ring[k, 3 - yl].astype(F32)
+            + ring[k, 5 - yl].astype(F32)
+        ).astype(BF16)
+        remote_copy(
+            own.at[k, j], pair.at[k], pair_send.at[k], pair_recv.at[k], **y_peer
+        ).start()
+
+    def gather_copy(k, m, lo, size, n, **device):
+        part = cols.at[k, m, pl.ds(lo, size)]
+        remote_copy(part, part, gather_send.at[k, n], gather_recv.at[k, n], **device).start()
+
+    def gather_arrived(k, size, n):
+        arrived(cols.at[k, 0, pl.ds(0, size)], gather_recv.at[k, n])
+
+    def e4(k):
+        arrived(pair.at[k], pair_recv.at[k])
+        cols[k, mp] = (
+            own[k, z * 2 + yl].astype(F32)
+            + ring[k, 2 + yl].astype(F32)
+            + ring[k, 4 + yl].astype(F32)
+            + pair[k].astype(F32)
+        ).astype(BF16)
+        gather_copy(k, mp, 0, rows, 0, **h_peer)
+        gather_copy(k, mp, 0, rows, 1, **x_next)
+        gather_copy(k, mp, 0, rows, 2, **x_prev)
+
+    def e5(k):
+        gather_arrived(k, rows, 0)
+        gather_copy(k, x * 2 + 1 - yh, 0, rows, 3, **x_next)
+        gather_copy(k, x * 2 + 1 - yh, 0, rows, 4, **x_prev)
+        gather_arrived(k, rows, 1)
+        gather_copy(k, xp * 2 + yh, 0, half, 5, **x_next)
+        gather_arrived(k, rows, 2)
+        gather_copy(k, xn * 2 + yh, half, half, 6, **x_prev)
+
+    def e6(k):
+        gather_arrived(k, rows, 3)
+        gather_copy(k, xp * 2 + 1 - yh, 0, half, 7, **x_next)
+        gather_arrived(k, rows, 4)
+        gather_copy(k, xn * 2 + 1 - yh, half, half, 8, **x_prev)
+
+    def e7(k):
+        for n in (5, 6, 7, 8):
+            gather_arrived(k, half, n)
+        for m in range(8):
+            local_copy(
+                cols.at[k, m],
+                cols_out.at[pl.ds(m * rows, rows), pl.ds(k * width, width)],
+                out_sem.at[1 + k],
+            ).start()
+
+    stages = (e1, e2, e3, e4, e5, e6, e7)
+    for s in range(chunks + len(stages) - 1):
+        for i, stage in enumerate(stages):
+            if 0 <= s - i < chunks:
+                stage(s - i)
+        if s == 0:
+            panel_forward()
+        if s == 1:
+            panel_share()
+
+    arrived(panel.at[0], panel_recv.at[7])
+    for i in range(2):
+        for j in range(8):
+            local_copy(
+                panel.at[i, j], panel_out.at[pl.ds((j * 2 + i) * 160, 160)], out_sem.at[0]
+            ).start()
+    arrived(panel, out_sem.at[0])
+    for n in range(7):
+        arrived(panel.at[0, 0], panel_send.at[n])
+    arrived(panel.at[0], panel_send.at[7])
+    for k in range(chunks):
+        arrived(swap.at[k], swap_send.at[k])
+        for slot in range(6):
+            arrived(ring.at[k, slot], ring_send.at[k, slot])
+        arrived(pair.at[k], pair_send.at[k])
+        for n in range(9):
+            arrived(cols.at[k, 0, pl.ds(0, rows if n < 5 else half)], gather_send.at[k, n])
+        arrived(cols.at[k], out_sem.at[1 + k])
+
+
+def gather(gradients, left_basis, chunks):
+    rows, block = gradients.shape[1], gradients.shape[2] // 16
+    width = block // chunks
+    depth, span = left_basis.shape
+    dma = pltpu.SemaphoreType.DMA
+    any_space = pl.BlockSpec(memory_space=pl.ANY)
+    return pl.pallas_call(
+        functools.partial(gather_kernel, chunks),
+        name="sum_and_gather",
+        out_shape=(
+            jax.ShapeDtypeStruct((rows * 8, block), BF16),
+            jax.ShapeDtypeStruct((depth * 16, span), BF16),
+        ),
+        in_specs=[any_space, any_space],
+        out_specs=(any_space, any_space),
+        scratch_shapes=[
+            pltpu.VMEM((chunks, 8, rows, width), BF16),
+            pltpu.VMEM((chunks, 8, rows, width), BF16),
+            pltpu.VMEM((chunks, 6, rows, width), BF16),
+            pltpu.VMEM((chunks, rows, width), BF16),
+            pltpu.VMEM((chunks, 8, rows, width), BF16),
+            pltpu.VMEM((2, 8, depth, span), BF16),
+            dma((chunks,)),
+            dma((chunks,)),
+            dma((chunks,)),
+            dma((chunks, 6)),
+            dma((chunks, 6)),
+            dma((chunks,)),
+            dma((chunks,)),
+            dma((chunks, 9)),
+            dma((chunks, 9)),
+            dma((8,)),
+            dma((8,)),
+            dma((1 + chunks,)),
+        ],
+        compiler_params=pltpu.CompilerParams(
+            collective_id=0, has_side_effects=True, vmem_limit_bytes=60 * 1024 * 1024
+        ),
+    )(gradients, left_basis)
+
 
 def on_device(
     gradients, left_basis, right_basis, first_moment, second_moment, left_stats, right_stats
 ):
-    summed = lax.psum_scatter(
-        gradients[0].astype(jnp.float32).astype(jnp.bfloat16), "dp", scatter_dimension=1, tiled=True
-    )
-    columns = lax.all_gather(summed, "mp", axis=0, tiled=True)
-    column_panel = lax.all_gather(left_basis, "dp", axis=0, tiled=True)
+    columns, column_panel = gather(gradients, left_basis, 4)
+    rows = gradients.shape[1]
+    summed = lax.dynamic_slice_in_dim(columns, lax.axis_index("mp") * rows, rows, 0)
     rotated = lax.dot_general(
         column_panel, columns, (((0,), (0,)), ((), ())), preferred_element_type=jnp.float32
     ).astype(jnp.bfloat16)

time: 415 us -> 280 us (0.67)
  waiting for transfers between devices: 363 us -> 133 us
  Pallas kernels: 0 us -> 102 us
  local copies, waits for them, and re-layouts: 8.99 us -> 2.08 us
    all_gather x2 -> x0, waiting for transfers between devices: 107 us -> none  [the longest x1 80.3 us: on_device(): columns = lax.all_gather(summed, 'mp', axis=0, tiled=True)]
    pallas_call x0 -> x1, Pallas kernels: none -> 102 us  [gather(): pl.pallas_call(functools.partial(gather_kernel, chunks), name='sum_and_ga...]
    unnamed x6 -> x2, waiting for transfers between devices: 94.7 us -> 0.03 us
    reduce_scatter x1, waiting for transfers between devices: 124 us -> 92.8 us  [on_device(): lax.psum_scatter(jnp.dot(column_panel, back, preferred_element_type=jnp.f...]
    unnamed x9 -> x8, local copies, waits for them, and re-layouts: 8.99 us -> 2.08 us
  transfers between devices with their start and end apart: 5 -> 2, of which waited for: 5 -> 2; matrix products, arithmetic and copies ran while one was open for 9% -> 8% of each run, Pallas kernels for 0% -> 0%
where the time goes in v1:
time: 280 us
  waiting for transfers between devices  133 us (48%)
  Pallas kernels  102 us (36%)
  matrix products  27.4 us (10%)
  between operations  14.1 us (5%)
    pallas_call x1, Pallas kernels, gather(): pl.pallas_call(functools.partial(gather_kernel, chunks), name='sum_and_ga...  102 us
    reduce_scatter x1, waiting for transfers between devices, on_device(): lax.psum_scatter(jnp.dot(column_panel, back, preferred_element_type=jnp.f...  92.8 us
    reduce_scatter x1, waiting for transfers between devices, on_device(): lax.psum_scatter(lax.dot_general(columns, summed, (((1,), (1,)), ((), ())...  40.2 us
    dot_general x1, matrix products, on_device(): jnp.dot(column_panel, back, preferred_element_type=jnp.float32)  8.38 us
    dot_general x1, matrix products, on_device(): turned = jnp.dot(rotated, block_basis, preferred_element_type=jnp.float32)  7.68 us
    dot_general x1, matrix products, on_device(): lax.dot_general(columns, summed, (((1,), (1,)), ((), ())), preferred_elem...  6.9 us
  transfers between devices with their start and end apart: 2, of which 2 were waited for; matrix products, arithmetic and copies ran while one was open for 8% of the time, Pallas kernels for 0%

profile of v1, /device:TPU:0, one launch (start us, length us, event | category | flops | bytes accessed | tf_op | source)
XLA Modules:
  0.0 280.1 jit_solution(8229960114628394043)
XLA Ops:
  7.2 0.0 copy-start
  7.2 0.0 reduce-scatter.5.cloned.1.call-start
  7.2 101.6 %sum_and_gather.1 = (bf16[2560,1024]{1,0:T(8,128)(2,1)}, bf16[2560,320]{1,0:T(8,128)(2,1)}) custom-call(bf16[1,320,16384]{2,1,0:T(8,128)(2,1)} %grads.1, bf16[160,320]{1,0:T(8,128)(2,1)} %left.1), custom_call_target="tpu_custom_call" | custom-call | tf_op jit(solution)/shard_map/sum_and_gather/pallas_call | solution.py:248
  108.8 6.9 %convolution_convert_fusion.1 = bf16[2560,320]{1,0:T(8,128)(2,1)} fusion(bf16[2560,1024]{1,0:T(8,128)(2,1)} %get-tuple-element.8, s32[]{:T(128)S(6)} %select_n.6), kind=kOutput, calls=%fused_computation.1 | convolution fusion | flops 1678540800 | bytes 7536644 | tf_op jit(solution)/shard_map/dot_general | solution.py:307
  115.7 0.0 copy-start.3
  115.7 0.0 reduce-scatter.5.cloned.1.call-update
  115.7 0.2 reduce-scatter.3.cloned.1.call-start
  116.0 0.0 copy-done
  116.0 1.1 copy-done.3
  117.0 7.7 %fusion.7 = (f32[320,1024]{1,0:T(8,128)}, f32[320,1024]{1,0:T(8,128)}) fusion(f32[320,1024]{1,0:T(8,128)S(1)} %copy-done.3, f32[320,1024]{1,0:T(8,128)} %param.10, bf16[1,1024,1024]{2,1,0:T(8,128)(2,1)S(1)} %copy-done, bf16[2560,320]{1,0:T(8,128)(2,1)} %get-tuple-element.7, bf16[2560,1024]{1,0:T(8,128)(2,1)} %get-tuple-element.8), kind=kOutput, calls=%fused_computation.9 | convolution fusion | flops 2351431680 | bytes 14221312 | tf_op jit(solution)/shard_map/dot_general | solution.py:293
  124.7 8.4 %convolution_convert_fusion = bf16[2560,1024]{1,0:T(8,128)(2,1)} fusion(bf16[2560,320]{1,0:T(8,128)(2,1)} %get-tuple-element.7, bf16[1,1024,1024]{2,1,0:T(8,128)(2,1)S(1)} %copy-done, f32[320,1024]{1,0:T(8,128)} %get-tuple-element.10, f32[320,1024]{1,0:T(8,128)} %get-tuple-element.9), kind=kOutput, calls=%fused_computation | convolution fusion | flops 2352742400 | bytes 11599872 | tf_op jit(solution)/shard_map/dot_general | solution.py:301
  133.1 0.0 copy-start.1
  133.1 0.0 reduce-scatter.3.cloned.1.call-update
  133.1 1.0 copy-done.1
  134.1 0.0 copy-start.2
  134.1 4.5 %fusion.9 = f32[1,128,1024]{2,1,0:T(8,128)} fusion(bf16[2560,1024]{1,0:T(8,128)(2,1)} %get-tuple-element.8, s32[]{:T(128)S(6)} %select_n.7, f32[1,128,1024]{2,1,0:T(8,128)S(1)} %copy-done.1), kind=kOutput, calls=%fused_computation.14 | convolution fusion | flops 671481856 | bytes 6946820 | tf_op jit(solution)/shard_map/dot_general | solution.py:318
  138.6 40.2 %reduce-scatter.5.cloned.1.call-done = bf16[160,320]{1,0:T(8,128)(2,1)} async-done(((bf16[2560,320]{1,0:T(8,128)(2,1)}), bf16[160,320]{1,0:T(8,128)(2,1)}) %reduce-scatter.5.cloned.1.call-update) | async-done | bytes 102416 | tf_op jit(solution)/shard_map/reduce_scatter | solution.py:306
  178.8 0.0 copy-done.2
  178.8 1.6 multiply_add_fusion.1
  180.5 92.8 %reduce-scatter.3.cloned.1.call-done = bf16[320,1024]{1,0:T(8,128)(2,1)} async-done(((bf16[2560,1024]{1,0:T(8,128)(2,1)}), bf16[320,1024]{1,0:T(8,128)(2,1)}) %reduce-scatter.3.cloned.1.call-update) | async-done | bytes 655376 | tf_op jit(solution)/shard_map/reduce_scatter | solution.py:300
Async XLA Ops:
  7.2 108.8 %copy-start = (bf16[1,1024,1024]{2,1,0:T(8,128)(2,1)S(1)}, bf16[1,1024,1024]{2,1,0:T(8,128)(2,1)}, u32[]{:S(2)}) copy-start(bf16[1,1024,1024]{2,1,0:T(8,128)(2,1)} %param.9) | copy-start | bytes 6291460
  7.2 171.6 %reduce-scatter.5.cloned.1.call-start = ((), (), s32[]{:S(2)}) async-start(), calls=%async_computation.3 | async-start | bytes 2088960 | tf_op jit(solution)/shard_map/reduce_scatter | solution.py:306
  115.7 1.3 copy-start.3
  115.7 157.6 %reduce-scatter.3.cloned.1.call-start = ((), (), s32[]{:S(2)}) async-start(), calls=%async_computation.2 | async-start | bytes 5898240 | tf_op jit(solution)/shard_map/reduce_scatter | solution.py:300
  133.1 1.0 copy-start.1
  134.1 44.7 %copy-start.2 = (f32[160,320]{1,0:T(8,128)S(1)}, f32[160,320]{1,0:T(8,128)}, u32[]{:S(2)}) copy-start(f32[160,320]{1,0:T(8,128)} %param.12) | copy-start | bytes 614404
Sparse Core Ops, SparseCore 0:
  115.9 62.9 reduce-scatter.4
  183.8 89.4 reduce-scatter.2

commit v2 on v1

v2 whole, which is shorter than its diff:
```python
import functools

import jax
import jax.numpy as jnp
from jax import lax
from jax.experimental import pallas as pl
from jax.experimental.pallas import tpu as pltpu
from jax.sharding import PartitionSpec as P

MESH = pl.DeviceIdType.MESH
beta_first = 0.9
beta_second = 0.95
beta_stats = 0.95
epsilon = 1e-08

F32 = jnp.float32
BF16 = jnp.bfloat16


def local_copy(src, dst, sem):
    return pltpu.make_async_copy(src, dst, sem)


def remote_copy(src, dst, send, recv, **device):
    return pltpu.make_async_remote_copy(
        src_ref=src,
        dst_ref=dst,
        send_sem=send,
        recv_sem=recv,
        device_id=device,
        device_id_type=MESH,
    )


def arrived(ref, sem):
    pltpu.make_async_copy(ref, ref, sem).wait()


def step_kernel(
    chunks, parts,
    grads, left, right, first, second, left_stats, right_stats,
    update_out, first_out, second_out, left_out, right_out,
    own, swap, ring, pair, cols, panel, panel_h, panel_t, panel_cat,
    basis, moment, square, turned, scaled, back_out, back, terms, terms_ring, halves, halves_out,
    outer, outer_swap, outer_ring, outer_pair, lstats, rstats, slice_t,
    load_sem, own_sem, swap_send, swap_recv, ring_send, ring_recv, pair_send, pair_recv,
    gather_send, gather_recv, panel_send, panel_recv, back_send, back_recv,
    terms_send, terms_recv, halves_send, halves_recv,
    outer_send, outer_recv, out_sem,
):
    dp = lax.axis_index("dp")
    mp = lax.axis_index("mp")
    z, yl, c = dp // 4, (dp // 2) % 2, dp % 2
    x, yh = mp // 2, mp % 2
    zn, zp, zo = (z + 1) % 4, (z + 3) % 4, (z + 2) % 4
    xn, xp, xo = (x + 1) % 4, (x + 3) % 4, (x + 2) % 4
    core_peer = {"dp": z * 4 + yl * 2 + (1 - c)}
    y_peer = {"dp": z * 4 + (1 - yl) * 2 + c}
    z_next = {"dp": zn * 4 + yl * 2 + c}
    z_prev = {"dp": zp * 4 + yl * 2 + c}
    h_peer = {"mp": x * 2 + (1 - yh)}
    x_next = {"mp": xn * 2 + yh}
    x_prev = {"mp": xp * 2 + yh}
    partners = (core_peer, y_peer, z_next, z_prev, h_peer, x_next, x_prev)

    rows, width = own.shape[2], own.shape[3]
    block = width * chunks
    half = rows // 2
    part = back.shape[2]
    hold = part * parts
    depth = panel.shape[2]

    def columns(owner, k):
        return pl.ds(pl.multiple_of(owner * block + k * width, 128), width)

    me = z * 2 + yl
    local_copy(left, panel.at[c, me], load_sem.at[0]).start()
    for k in range(chunks):
        for j in range(8):
            local_copy(
                grads.at[0, :, columns(j * 2 + c, k)], own.at[k, j], own_sem.at[k]
            ).start()

    barrier = pltpu.get_barrier_semaphore()
    for p in partners:
        pl.semaphore_signal(barrier, inc=1, device_id=p, device_id_type=MESH)
    pl.semaphore_wait(barrier, len(partners))

    for k in range(chunks):
        for j in range(8):
            remote_copy(
                grads.at[0, :, columns(j * 2 + 1 - c, k)], swap.at[k, j],
                swap_send.at[k], swap_recv.at[k], **core_peer,
            ).start()

    local_copy(right.at[0], basis, load_sem.at[1]).start()
    local_copy(first, moment, load_sem.at[2]).start()
    local_copy(second, square, load_sem.at[3]).start()
    local_copy(left_stats, lstats, load_sem.at[4]).start()
    local_copy(right_stats.at[0], rstats, load_sem.at[5]).start()

    arrived(panel.at[0, 0], load_sem.at[0])

    def panel_copy(slot, n, **device):
        return remote_copy(
            panel.at[c, slot], panel.at[c, slot], panel_send.at[n], panel_recv.at[n], **device
        )

    panel_copy(me, 0, **y_peer).start()
    panel_copy(me, 1, **z_next).start()
    panel_copy(me, 2, **z_prev).start()

    def panel_forward():
        one = panel.at[0, 0]
        arrived(one, panel_recv.at[0])
        other = z * 2 + 1 - yl
        panel_copy(other, 3, **z_next).start()
        panel_copy(other, 4, **z_prev).start()
        arrived(one, panel_recv.at[1])
        panel_copy(zp * 2 + yl, 5, **z_next).start()
        arrived(one, panel_recv.at[2])
        arrived(one, panel_recv.at[4])
        panel_copy(zn * 2 + 1 - yl, 6, **z_prev).start()

    def panel_share():
        one = panel.at[0, 0]
        for n in (3, 5, 6):
            arrived(one, panel_recv.at[n])
        remote_copy(
            panel.at[c], panel.at[c], panel_send.at[7], panel_recv.at[7], **core_peer
        ).start()
        remote_copy(
            panel.at[c], panel_h.at[c], panel_send.at[8], panel_recv.at[8], **h_peer
        ).start()

    def panel_turn():
        arrived(panel.at[0], panel_recv.at[7])
        for i in range(4):
            four = jnp.concatenate(
                [panel[0, 2 * i], panel[1, 2 * i], panel[0, 2 * i + 1], panel[1, 2 * i + 1]], axis=0
            )
            panel_t[:, pl.ds(i * 4 * depth, 4 * depth)] = four.T

    def panel_share_h():
        arrived(panel.at[0], panel_recv.at[8])
        remote_copy(
            panel_h.at[c], panel_h.at[c], panel_send.at[9], panel_recv.at[9], **core_peer
        ).start()

    def panel_join():
        arrived(panel.at[0], panel_recv.at[9])

        def join(j, carry):
            for i in range(2):
                panel_cat[j, pl.ds(i * depth, depth)] = jnp.concatenate(
                    [panel[i, j], panel_h[i, j]], axis=1
                )
            return carry

        lax.fori_loop(0, 8, join, 0)

    def ring_stages(own, ring, send, recv, now, nxt, prv, opp, to_next, to_prev):
        def copy(j, slot, device):
            remote_copy(own.at[j], ring.at[slot], send.at[slot], recv.at[slot], **device).start()

        def first_stage(term):
            term(opp * 2)
            copy(opp * 2, 0, to_next)
            term(opp * 2 + 1)
            copy(opp * 2 + 1, 1, to_prev)
            term(nxt * 2 + 1)
            copy(nxt * 2 + 1, 3, to_next)
            term(prv * 2)
            copy(prv * 2, 4, to_prev)
            term(nxt * 2)
            term(prv * 2 + 1)
            term(now * 2)
            term(now * 2 + 1)

        def second_stage():
            arrived(ring.at[0], recv.at[0])
            j = nxt * 2
            own[j] = (own[j].astype(F32) + ring[0].astype(F32)).astype(BF16)
            copy(j, 2, to_next)
            arrived(ring.at[1], recv.at[1])
            i = prv * 2 + 1
            own[i] = (own[i].astype(F32) + ring[1].astype(F32)).astype(BF16)
            copy(i, 5, to_prev)

        def third_stage():
            for slot in (3, 4, 2, 5):
                arrived(ring.at[slot], recv.at[slot])

        def total(which):
            return (
                own[now * 2 + which].astype(F32)
                + ring[2 + which].astype(F32)
                + ring[4 + which].astype(F32)
            )

        def sent():
            for slot in range(6):
                arrived(ring.at[slot], send.at[slot])

        return first_stage, second_stage, third_stage, total, sent

    grad_rings = [
        ring_stages(
            own.at[k], ring.at[k], ring_send.at[k], ring_recv.at[k],
            z, zn, zp, zo, z_next, z_prev,
        )
        for k in range(chunks)
    ]

    def e1(k):
        arrived(own.at[k], own_sem.at[k])
        arrived(swap.at[k], swap_recv.at[k])

        def add(j):
            own[k, j] = (own[k, j].astype(F32) + swap[k, j].astype(F32)).astype(BF16)

        grad_rings[k][0](add)

    def e2(k):
        grad_rings[k][1]()

    def e3(k):
        grad_rings[k][2]()
        j = z * 2 + 1 - yl
        own[k, j] = grad_rings[k][3](1 - yl).astype(BF16)
        remote_copy(
            own.at[k, j], pair.at[k], pair_send.at[k], pair_recv.at[k], **y_peer
        ).start()

    def gather_copy(k, m, lo, size, n, **device):
        piece = cols.at[k, m, pl.ds(lo, size)]
        remote_copy(piece, piece, gather_send.at[k, n], gather_recv.at[k, n], **device).start()

    def gather_arrived(k, size, n):
        arrived(cols.at[k, 0, pl.ds(0, size)], gather_recv.at[k, n])

    def e4(k):
        arrived(pair.at[k], pair_recv.at[k])
        cols[k, mp] = (grad_rings[k][3](yl) + pair[k].astype(F32)).astype(BF16)
        gather_copy(k, mp, 0, rows, 0, **h_peer)
        gather_copy(k, mp, 0, rows, 1, **x_next)
        gather_copy(k, mp, 0, rows, 2, **x_prev)

    def e5(k):
        gather_arrived(k, rows, 0)
        gather_copy(k, x * 2 + 1 - yh, 0, rows, 3, **x_next)
        gather_copy(k, x * 2 + 1 - yh, 0, rows, 4, **x_prev)
        gather_arrived(k, rows, 1)
        gather_copy(k, xp * 2 + yh, 0, half, 5, **x_next)
        gather_arrived(k, rows, 2)
        gather_copy(k, xn * 2 + yh, half, half, 6, **x_prev)

    def e6(k):
        gather_arrived(k, rows, 3)
        gather_copy(k, xp * 2 + 1 - yh, 0, half, 7, **x_next)
        gather_arrived(k, rows, 4)
        gather_copy(k, xn * 2 + 1 - yh, half, half, 8, **x_prev)

    def e7(k):
        for n in (5, 6, 7, 8):
            gather_arrived(k, half, n)
        rotated = jnp.dot(
            panel_t[...], cols[k].reshape(8 * rows, width), preferred_element_type=F32
        ).astype(BF16)
        if k == 0:
            arrived(basis, load_sem.at[1])
        for n in range(4):
            at = pl.ds(n * (block // 4), block // 4)
            term = jnp.dot(
                rotated, basis[pl.ds(k * width, width), at], preferred_element_type=F32
            )
            turned[:, at] = term if k == 0 else turned[:, at] + term

    stages = (e1, e2, e3, e4, e5, e6, e7)
    for s in range(chunks + len(stages) - 1):
        for i, stage in enumerate(stages):
            if 0 <= s - i < chunks:
                stage(s - i)
        if s == 0:
            panel_forward()
        if s == 1:
            panel_share()
        if s == 2:
            panel_turn()
        if s == 3:
            panel_share_h()
        if s == 4:
            panel_join()

    arrived(moment, load_sem.at[2])
    arrived(square, load_sem.at[3])

    def moments(i, carry):
        at = pl.ds(pl.multiple_of(i * 32, 32), 32)
        t = turned[at]
        new_first = beta_first * moment[at] + (1.0 - beta_first) * t
        new_second = beta_second * square[at] + (1.0 - beta_second) * t * t
        moment[at] = new_first
        square[at] = new_second
        scaled[at] = (new_first / (jnp.sqrt(new_second) + epsilon)).astype(BF16)
        return carry

    lax.fori_loop(0, rows // 32, moments, 0)
    local_copy(moment, first_out, out_sem.at[0]).start()
    local_copy(square, second_out, out_sem.at[1]).start()

    def back_part(which, k):
        at = pl.ds(pl.multiple_of(which * hold + k * part, 128), part)
        return lax.dot_general(
            scaled[...], basis[at], (((1,), (1,)), ((), ())), preferred_element_type=F32
        ).astype(BF16)

    for k in range(parts):
        back_out[k] = back_part(1 - yh, k)
        remote_copy(
            back_out.at[k], back.at[k, pl.ds(rows, rows)], back_send.at[k], back_recv.at[k],
            **h_peer,
        ).start()
    for k in range(parts):
        back[k, pl.ds(0, rows)] = back_part(yh, k)

    def outer_terms(j, carry):
        total = jnp.zeros((rows, rows), F32)
        for k in range(chunks):
            total += lax.dot_general(
                cols[k, j], cols[k, mp], (((1,), (1,)), ((), ())), preferred_element_type=F32
            )
        outer[0, j] = total[:half].astype(BF16)
        outer[1, j] = total[half:].astype(BF16)
        return carry

    def outer_start():
        lax.fori_loop(0, 8, outer_terms, 0)
        remote_copy(
            outer.at[1 - c], outer_swap, outer_send.at[6], outer_recv.at[6], **core_peer
        ).start()

    outer_ring_stages = ring_stages(
        outer.at[c], outer_ring, outer_send, outer_recv, z, zn, zp, zo, z_next, z_prev
    )

    def l1():
        arrived(outer_swap, outer_recv.at[6])

        def add(j):
            outer[c, j] = (outer[c, j].astype(F32) + outer_swap[j].astype(F32)).astype(BF16)

        outer_ring_stages[0](add)

    def l2():
        outer_ring_stages[1]()

    def l3():
        outer_ring_stages[2]()
        j = z * 2 + 1 - yl
        outer[c, j] = outer_ring_stages[3](1 - yl).astype(BF16)
        remote_copy(
            outer.at[c, j], outer_pair, outer_send.at[7], outer_recv.at[7], **y_peer
        ).start()

    def l4():
        arrived(outer_pair, outer_recv.at[7])
        arrived(lstats, load_sem.at[4])
        total = outer_ring_stages[3](yl) + outer_pair[...].astype(F32)
        lstats[...] = beta_stats * lstats[...] + (1.0 - beta_stats) * total
        local_copy(lstats, left_out, out_sem.at[2]).start()

    def right_terms():
        share = rstats.shape[0]
        k_own = (mp * share) // width
        off = pl.ds(pl.multiple_of((mp * share) % width, 128), share)
        for i in range(4):
            two = cols[k_own, pl.ds(2 * i, 2), :, off].reshape(2 * rows, share)
            slice_t[:, pl.ds(i * 2 * rows, 2 * rows)] = two.T
        arrived(rstats, load_sem.at[5])
        for k in range(chunks):
            at = pl.ds(k * width, width)
            term = jnp.dot(
                slice_t[...], cols[k].reshape(8 * rows, width), preferred_element_type=F32
            )
            rstats[:, at] = beta_stats * rstats[:, at] + (1.0 - beta_stats) * term
        local_copy(rstats, right_out.at[0], out_sem.at[3]).start()

    term_rings = [
        ring_stages(
            terms.at[k], terms_ring.at[k], terms_send.at[k], terms_recv.at[k],
            x, xn, xp, xo, x_next, x_prev,
        )
        for k in range(parts)
    ]

    def u1(k):
        arrived(back.at[k, pl.ds(0, rows)], back_recv.at[k])

        def term(j):
            terms[k, j] = jnp.dot(
                panel_cat[j], back[k], preferred_element_type=F32
            ).astype(BF16)

        term_rings[k][0](term)

    def u2(k):
        term_rings[k][1]()

    def u3(k):
        term_rings[k][2]()
        halves_out[k] = term_rings[k][3](1 - yh).astype(BF16)
        remote_copy(
            halves_out.at[k], halves.at[yh, k], halves_send.at[k], halves_recv.at[k], **h_peer
        ).start()
        halves[yh, k] = term_rings[k][3](yh).astype(BF16)
        local_copy(
            halves.at[yh, k],
            update_out.at[:, pl.ds(pl.multiple_of(yh * hold + k * part, 128), part)],
            out_sem.at[4],
        ).start()

    def u4(k):
        arrived(halves.at[0, k], halves_recv.at[k])
        local_copy(
            halves.at[1 - yh, k],
            update_out.at[:, pl.ds(pl.multiple_of((1 - yh) * hold + k * part, 128), part)],
            out_sem.at[5],
        ).start()

    extras = {0: (outer_start,), 1: (l1,), 2: (l2, right_terms), 3: (l3,), 4: (l4,)}
    late = (u1, u2, u3, u4)
    for s in range(max(parts + len(late) - 1, 5)):
        for i, stage in enumerate(late):
            if 0 <= s - i < parts:
                stage(s - i)
        for extra in extras.get(s, ()):
            extra()

    for n in range(7):
        arrived(panel.at[0, 0], panel_send.at[n])
    for n in range(7, 10):
        arrived(panel.at[0], panel_send.at[n])
    for k in range(chunks):
        arrived(swap.at[k], swap_send.at[k])
        grad_rings[k][4]()
        arrived(pair.at[k], pair_send.at[k])
        for n in range(9):
            arrived(cols.at[k, 0, pl.ds(0, rows if n < 5 else half)], gather_send.at[k, n])
    for k in range(parts):
        arrived(back_out.at[k], back_send.at[k])
        term_rings[k][4]()
        arrived(halves_out.at[k], halves_send.at[k])
    outer_ring_stages[4]()
    arrived(outer_swap, outer_send.at[6])
    arrived(outer_pair, outer_send.at[7])
    arrived(moment, out_sem.at[0])
    arrived(square, out_sem.at[1])
    arrived(lstats, out_sem.at[2])
    arrived(rstats, out_sem.at[3])
    arrived(halves.at[0], out_sem.at[4])
    arrived(halves.at[0], out_sem.at[5])


def on_device(
    gradients, left_basis, right_basis, first_moment, second_moment, left_stats, right_stats,
    chunks=4, parts=4,
):
    rows, block = gradients.shape[1], gradients.shape[2] // 16
    width = block // chunks
    part = block // 2 // parts
    depth, span = left_basis.shape
    share = right_stats.shape[1]
    dma = pltpu.SemaphoreType.DMA
    any_space = pl.BlockSpec(memory_space=pl.ANY)

    def buffer(*shape, dtype=BF16):
        return pltpu.VMEM(shape, dtype)

    return pl.pallas_call(
        functools.partial(step_kernel, chunks, parts),
        name="soap_step",
        out_shape=(
            jax.ShapeDtypeStruct((rows, block), BF16),
            jax.ShapeDtypeStruct((rows, block), F32),
            jax.ShapeDtypeStruct((rows, block), F32),
            jax.ShapeDtypeStruct((depth, span), F32),
            jax.ShapeDtypeStruct((1, share, block), F32),
        ),
        in_specs=[any_space] * 7,
        out_specs=(any_space,) * 5,
        scratch_shapes=[
            buffer(chunks, 8, rows, width),
            buffer(chunks, 8, rows, width),
            buffer(chunks, 6, rows, width),
            buffer(chunks, rows, width),
            buffer(chunks, 8, rows, width),
            buffer(2, 8, depth, span),
            buffer(2, 8, depth, span),
            buffer(span, 16 * depth),
            buffer(8, 2 * depth, 2 * span),
            buffer(block, block),
            buffer(rows, block, dtype=F32),
            buffer(rows, block, dtype=F32),
            buffer(rows, block, dtype=F32),
            buffer(rows, block),
            buffer(parts, rows, part),
            buffer(parts, 2 * rows, part),
            buffer(parts, 8, rows, part),
            buffer(parts, 6, rows, part),
            buffer(2, parts, rows, part),
            buffer(parts, rows, part),
            buffer(2, 8, depth, span),
            buffer(8, depth, span),
            buffer(6, depth, span),
            buffer(depth, span),
            buffer(depth, span, dtype=F32),
            buffer(share, block, dtype=F32),
            buffer(share, 8 * rows),
            dma((6,)),
            dma((chunks,)),
            dma((chunks,)),
            dma((chunks,)),
            dma((chunks, 6)),
            dma((chunks, 6)),
            dma((chunks,)),
            dma((chunks,)),
            dma((chunks, 9)),
            dma((chunks, 9)),
            dma((10,)),
            dma((10,)),
            dma((parts,)),
            dma((parts,)),
            dma((parts, 6)),
            dma((parts, 6)),
            dma((parts,)),
            dma((parts,)),
            dma((8,)),
            dma((8,)),
            dma((6,)),
        ],
        compiler_params=pltpu.CompilerParams(
            collective_id=0, has_side_effects=True, vmem_limit_bytes=62 * 1024 * 1024
        ),
    )(gradients, left_basis, right_basis, first_moment, second_moment, left_stats, right_stats)


def solution(mesh):
    return jax.shard_map(
        on_device,
        mesh=mesh,
        in_specs=(
            P("dp", "mp", None),
            P("dp", "mp"),
            P("dp", None, None),
            P("mp", "dp"),
            P("mp", "dp"),
            P("dp", "mp"),
            P("dp", "mp", None),
        ),
        out_specs=(P("mp", "dp"), P("mp", "dp"), P("mp", "dp"), P("dp", "mp"), P("dp", "mp", None)),
        check_vma=False,
    )
```

time: 280 us -> 146 us (0.52)
  waiting for transfers between devices: 133 us -> 0 us
  Pallas kernels: 102 us -> 139 us
  matrix products: 27.4 us -> 0 us
  between operations: 14.1 us -> 0.66 us
  local copies, waits for them, and re-layouts: 2.08 us -> 6.53 us
    reduce_scatter x2 -> x0, waiting for transfers between devices: 133 us -> none  [the longest x1 92.8 us: on_device(): lax.psum_scatter(jnp.dot(column_panel, back, preferred_element_type=jnp.f...]
    pallas_call x1, Pallas kernels: 102 us -> 139 us  [on_device(): pl.pallas_call(functools.partial(step_kernel, chunks, parts), name='soap_...]
    dot_general x4 -> x0, matrix products: 27.4 us -> none  [the longest x1 8.38 us: on_device(): jnp.dot(column_panel, back, preferred_element_type=jnp.float32)]
    unnamed x8 -> x13, local copies, waits for them, and re-layouts: 2.08 us -> 6.53 us
  transfers between devices with their start and end apart: 2 -> 0, of which waited for: 2 -> 0; matrix products, arithmetic and copies ran while one was open for 8% -> 0% of each run, Pallas kernels for 0% -> 0%
where the time goes in v2:
time: 146 us
  Pallas kernels  139 us (95%)
  local copies, waits for them, and re-layouts  6.53 us (4%)
    pallas_call x1, Pallas kernels, on_device(): pl.pallas_call(functools.partial(step_kernel, chunks, parts), name='soap_...  139 us
    unnamed x13, local copies, waits for them, and re-layouts  6.53 us

profile of v2, /device:TPU:0, one launch (start us, length us, event | category | flops | bytes accessed | tf_op | source)
XLA Modules:
  0.0 145.9 jit_solution(11195265702914659123)
XLA Ops:
  0.6 138.7 %soap_step.1 = (bf16[320,1024]{1,0:T(8,128)(2,1)}, f32[320,1024]{1,0:T(8,128)}, f32[320,1024]{1,0:T(8,128)}, f32[160,320]{1,0:T(8,128)}, f32[1,128,1024]{2,1,0:T(8,128)}) custom-call(bf16[1,320,16384]{2,1,0:T(8,128)(2,1)} %grads.1, bf16[160,320]{1,0:T(8,128)(2,1)} %left.1, bf16[1,1024,1024]{2,1,0:T(8,128)(2,1)} %right.1, f32[320,1024]{1,0:T(8,128)} %first.1, ...), custom_call_target="tpu_custom_call" | custom-call | tf_op jit(solution)/shard_map/soap_step/pallas_call | solution.py:480
  139.3 0.0 copy-start.1
  139.3 2.1 %copy.17 = bf16[320,1024]{1,0:T(8,128)(2,1)} copy(bf16[320,1024]{1,0:T(8,128)(2,1)} %get-tuple-element.10) | data formatting | bytes 1310720
  141.4 0.0 copy-done.1
  141.4 0.0 copy-start
  141.4 1.1 copy.18
  142.5 0.7 copy-done
  143.2 0.0 copy-start.3
  143.2 0.0 copy-start.2
  143.2 1.1 copy.19
  144.3 0.1 copy-done.3
  144.4 0.7 copy.20
  145.1 0.0 copy-done.2
  145.1 0.8 copy.21
Async XLA Ops:
  139.3 2.1 %copy-start.1 = (f32[320,1024]{1,0:T(8,128)S(1)}, f32[320,1024]{1,0:T(8,128)}, u32[]{:S(2)}) copy-start(f32[320,1024]{1,0:T(8,128)} %get-tuple-element.11) | copy-start | bytes 3932164
  141.4 1.8 %copy-start = (f32[320,1024]{1,0:T(8,128)S(1)}, f32[320,1024]{1,0:T(8,128)}, u32[]{:S(2)}) copy-start(f32[320,1024]{1,0:T(8,128)} %get-tuple-element.12) | copy-start | bytes 3932164
  143.2 1.2 copy-start.3
  143.2 1.9 %copy-start.2 = (f32[1,128,1024]{2,1,0:T(8,128)S(1)}, f32[1,128,1024]{2,1,0:T(8,128)}, u32[]{:S(2)}) copy-start(f32[1,128,1024]{2,1,0:T(8,128)} %get-tuple-element.14) | copy-start | bytes 1572868

commit v3 on v2

--- a/solution.py
+++ b/solution.py
@@ -1,3 +1,4 @@
+import collections
 import functools
 
 import jax
@@ -36,8 +37,51 @@
     pltpu.make_async_copy(ref, ref, sem).wait()
 
 
+PLACES = (
+    (0, 0, 320), (1, 0, 320), (2, 0, 320), (3, 0, 320), (4, 0, 320), (5, 0, 320),
+    (6, 0, 320), (7, 0, 320),
+)
+
+ORDER = (
+    (
+        ("e1", 0), ("e1b", 0), ("e1c", 0), ("panel_f1", 0), ("e1", 1), ("e2", 0), ("panel_f2", 0),
+        ("e1b", 1), ("e1c", 1), ("e2", 1), ("e3", 0), ("e1", 2), ("panel_share", 0),
+        ("panel_h", 0), ("e1b", 2), ("e1c", 2), ("e3", 1), ("e1", 3), ("e4", 0),
+        ("panel_turn", 0), ("e2", 2), ("panel_h", 1), ("e1b", 3), ("e1c", 3), ("e4", 1),
+        ("e5", 0), ("e2", 3), ("e5b", 0), ("e3", 2), ("e1", 4), ("panel_h", 2), ("e5", 1),
+        ("e1b", 4), ("e1c", 4), ("e5b", 1), ("panel_h", 3), ("e3", 3), ("e1", 5), ("e4", 2),
+        ("e6", 0), ("e2", 4), ("e6", 1), ("e1b", 5), ("e1c", 5), ("panel_h", 4), ("e4", 3),
+        ("e5", 2), ("e2", 5), ("e7", 0), ("e5b", 2), ("e3", 4), ("e1", 6), ("e7", 1),
+        ("panel_h", 5), ("e5", 3), ("e1b", 6), ("e1c", 6), ("e3", 5), ("e1", 7), ("e5b", 3),
+        ("panel_h", 6), ("e6", 2), ("e4", 4), ("e2", 6), ("e1b", 7), ("e1c", 7), ("e4", 5),
+        ("e6", 3), ("e2", 7), ("e7", 2), ("e3", 6), ("panel_h", 7), ("e5", 4), ("e5b", 4),
+        ("e5", 5), ("e5b", 5), ("e7", 3), ("e3", 7), ("e4", 6), ("panel_share_h", 0), ("e6", 4),
+        ("e6", 5), ("e4", 7), ("panel_join", 0), ("e5", 6), ("e5b", 6), ("e7", 4), ("e7", 5),
+        ("e5b", 7), ("e5", 7), ("e6", 6), ("e6", 7), ("e7", 6), ("e7", 7),
+    ),
+    (
+        ("bo", 0), ("bo", 1), ("bo", 2), ("bo", 3), ("bi", 0), ("bi", 1), ("bi", 2), ("bi", 3),
+        ("outer", 0), ("outer", 1), ("outer", 2), ("u1", 0), ("outer", 3), ("u1b", 0), ("u1c", 0),
+        ("outer_send", 0), ("right", 0), ("u1", 1), ("u2", 0), ("l1", 0), ("u1b", 1), ("u1c", 1),
+        ("u2", 1), ("u3", 0), ("u1", 2), ("l2", 0), ("u1b", 2), ("u1c", 2), ("u3", 1), ("u1", 3),
+        ("u4", 0), ("u2", 2), ("l3", 0), ("u1b", 3), ("u1c", 3), ("u4", 1), ("u2", 3), ("u3", 2),
+        ("l4", 0), ("u3", 3), ("u4", 2), ("u4", 3),
+    ),
+)
+
+
+RingSum = collections.namedtuple(
+    "RingSum", ("far", "near", "rest", "second", "third", "total", "sent")
+)
+
+
+def run(order, **stages):
+    for name, k in order:
+        stages[name](k)
+
+
 def step_kernel(
-    chunks, parts,
+    places, parts, order,
     grads, left, right, first, second, left_stats, right_stats,
     update_out, first_out, second_out, left_out, right_out,
     own, swap, ring, pair, cols, panel, panel_h, panel_t, panel_cat,
@@ -59,11 +103,13 @@
     z_next = {"dp": zn * 4 + yl * 2 + c}
     z_prev = {"dp": zp * 4 + yl * 2 + c}
     h_peer = {"mp": x * 2 + (1 - yh)}
+    q_peer = {"dp": z * 4 + (1 - yl) * 2 + c, "mp": x * 2 + (1 - yh)}
     x_next = {"mp": xn * 2 + yh}
     x_prev = {"mp": xp * 2 + yh}
-    partners = (core_peer, y_peer, z_next, z_prev, h_peer, x_next, x_prev)
+    partners = (core_peer, y_peer, z_next, z_prev, h_peer, q_peer, x_next, x_prev)
 
     rows, width = own.shape[2], own.shape[3]
+    chunks = own.shape[0]
     block = width * chunks
     half = rows // 2
     part = back.shape[2]
@@ -75,10 +121,15 @@
 
     me = z * 2 + yl
     local_copy(left, panel.at[c, me], load_sem.at[0]).start()
-    for k in range(chunks):
+    def piece(ref, i):
+        k, lo, size = places[i]
+        return ref.at[k, :, pl.ds(lo, size)]
+
+    for i, (k, lo, size) in enumerate(places):
         for j in range(8):
             local_copy(
-                grads.at[0, :, columns(j * 2 + c, k)], own.at[k, j], own_sem.at[k]
+                grads.at[0, pl.ds(lo, size), columns(j * 2 + c, k)],
+                own.at[k, j, pl.ds(lo, size)], own_sem.at[i],
             ).start()
 
     barrier = pltpu.get_barrier_semaphore()
@@ -86,11 +137,23 @@
         pl.semaphore_signal(barrier, inc=1, device_id=p, device_id_type=MESH)
     pl.semaphore_wait(barrier, len(partners))
 
-    for k in range(chunks):
+    arrived(panel.at[0, 0], load_sem.at[0])
+
+    def panel_copy(slot, n, **device):
+        return remote_copy(
+            panel.at[c, slot], panel.at[c, slot], panel_send.at[n], panel_recv.at[n], **device
+        )
+
+    panel_copy(me, 0, **y_peer).start()
+    panel_copy(me, 1, **z_next).start()
+    panel_copy(me, 2, **z_prev).start()
+
+    for i, (k, lo, size) in enumerate(places):
         for j in range(8):
             remote_copy(
-                grads.at[0, :, columns(j * 2 + 1 - c, k)], swap.at[k, j],
-                swap_send.at[k], swap_recv.at[k], **core_peer,
+                grads.at[0, pl.ds(lo, size), columns(j * 2 + 1 - c, k)],
+                swap.at[k, j, pl.ds(lo, size)],
+                swap_send.at[i], swap_recv.at[i], **core_peer,
             ).start()
 
     local_copy(right.at[0], basis, load_sem.at[1]).start()
@@ -99,38 +162,35 @@
     local_copy(left_stats, lstats, load_sem.at[4]).start()
     local_copy(right_stats.at[0], rstats, load_sem.at[5]).start()
 
-    arrived(panel.at[0, 0], load_sem.at[0])
-
-    def panel_copy(slot, n, **device):
-        return remote_copy(
-            panel.at[c, slot], panel.at[c, slot], panel_send.at[n], panel_recv.at[n], **device
-        )
-
-    panel_copy(me, 0, **y_peer).start()
-    panel_copy(me, 1, **z_next).start()
-    panel_copy(me, 2, **z_prev).start()
+    one = panel.at[0, 0]
+
+    def panel_part(slot, lo, n, **device):
+        piece = panel.at[c, slot, pl.ds(lo, depth // 2)]
+        remote_copy(piece, piece, panel_send.at[n], panel_recv.at[n], **device).start()
 
     def panel_forward():
-        one = panel.at[0, 0]
-        arrived(one, panel_recv.at[0])
-        other = z * 2 + 1 - yl
-        panel_copy(other, 3, **z_next).start()
-        panel_copy(other, 4, **z_prev).start()
         arrived(one, panel_recv.at[1])
-        panel_copy(zp * 2 + yl, 5, **z_next).start()
+        panel_part(zp * 2 + yl, 0, 3, **z_next)
+        panel_copy(zp * 2 + yl, 5, **y_peer).start()
         arrived(one, panel_recv.at[2])
-        arrived(one, panel_recv.at[4])
-        panel_copy(zn * 2 + 1 - yl, 6, **z_prev).start()
+        panel_part(zn * 2 + yl, depth // 2, 4, **z_prev)
+        panel_copy(zn * 2 + yl, 6, **y_peer).start()
+
+    def panel_forward_far():
+        for n in (3, 4):
+            arrived(panel.at[0, 0, pl.ds(0, depth // 2)], panel_recv.at[n])
+        panel_copy(zo * 2 + yl, 17, **y_peer).start()
 
     def panel_share():
-        one = panel.at[0, 0]
-        for n in (3, 5, 6):
+        for n in (0, 5, 6, 17):
             arrived(one, panel_recv.at[n])
         remote_copy(
             panel.at[c], panel.at[c], panel_send.at[7], panel_recv.at[7], **core_peer
         ).start()
-        remote_copy(
-            panel.at[c], panel_h.at[c], panel_send.at[8], panel_recv.at[8], **h_peer
+
+    def panel_h_copy(j):
+        remote_copy(
+            panel.at[c, j], panel_h.at[c, j], panel_send.at[9 + j], panel_recv.at[9 + j], **q_peer
         ).start()
 
     def panel_turn():
@@ -142,13 +202,14 @@
             panel_t[:, pl.ds(i * 4 * depth, 4 * depth)] = four.T
 
     def panel_share_h():
+        for j in range(8):
+            arrived(panel.at[0, 0], panel_recv.at[9 + j])
+        remote_copy(
+            panel_h.at[c], panel_h.at[c], panel_send.at[8], panel_recv.at[8], **core_peer
+        ).start()
+
+    def panel_join():
         arrived(panel.at[0], panel_recv.at[8])
-        remote_copy(
-            panel_h.at[c], panel_h.at[c], panel_send.at[9], panel_recv.at[9], **core_peer
-        ).start()
-
-    def panel_join():
-        arrived(panel.at[0], panel_recv.at[9])
 
         def join(j, carry):
             for i in range(2):
@@ -163,15 +224,19 @@
         def copy(j, slot, device):
             remote_copy(own.at[j], ring.at[slot], send.at[slot], recv.at[slot], **device).start()
 
-        def first_stage(term):
+        def far_stage(term):
             term(opp * 2)
             copy(opp * 2, 0, to_next)
             term(opp * 2 + 1)
             copy(opp * 2 + 1, 1, to_prev)
+
+        def near_stage(term):
             term(nxt * 2 + 1)
             copy(nxt * 2 + 1, 3, to_next)
             term(prv * 2)
             copy(prv * 2, 4, to_prev)
+
+        def rest_stage(term):
             term(nxt * 2)
             term(prv * 2 + 1)
             term(now * 2)
@@ -202,68 +267,97 @@
             for slot in range(6):
                 arrived(ring.at[slot], send.at[slot])
 
-        return first_stage, second_stage, third_stage, total, sent
+        return RingSum(far_stage, near_stage, rest_stage, second_stage, third_stage, total, sent)
 
     grad_rings = [
         ring_stages(
-            own.at[k], ring.at[k], ring_send.at[k], ring_recv.at[k],
+            piece(own, i), piece(ring, i), ring_send.at[i], ring_recv.at[i],
             z, zn, zp, zo, z_next, z_prev,
         )
-        for k in range(chunks)
+        for i in range(len(places))
     ]
 
-    def e1(k):
-        arrived(own.at[k], own_sem.at[k])
-        arrived(swap.at[k], swap_recv.at[k])
+    def e1_term(i):
+        mine, theirs = piece(own, i), piece(swap, i)
 
         def add(j):
-            own[k, j] = (own[k, j].astype(F32) + swap[k, j].astype(F32)).astype(BF16)
-
-        grad_rings[k][0](add)
-
-    def e2(k):
-        grad_rings[k][1]()
-
-    def e3(k):
-        grad_rings[k][2]()
+            mine[j] = (mine[j].astype(F32) + theirs[j].astype(F32)).astype(BF16)
+
+        return add
+
+    def e1(i):
+        arrived(piece(own, i), own_sem.at[i])
+        arrived(piece(swap, i), swap_recv.at[i])
+        grad_rings[i].far(e1_term(i))
+
+    def e1b(i):
+        grad_rings[i].near(e1_term(i))
+
+    def e1c(i):
+        grad_rings[i].rest(e1_term(i))
+
+    def e2(i):
+        grad_rings[i].second()
+
+    def pair_piece(i):
+        k, lo, size = places[i]
+        return pair.at[k, pl.ds(lo, size)]
+
+    def e3(i):
+        grad_rings[i].third()
+        mine = piece(own, i)
         j = z * 2 + 1 - yl
-        own[k, j] = grad_rings[k][3](1 - yl).astype(BF16)
-        remote_copy(
-            own.at[k, j], pair.at[k], pair_send.at[k], pair_recv.at[k], **y_peer
-        ).start()
-
-    def gather_copy(k, m, lo, size, n, **device):
-        piece = cols.at[k, m, pl.ds(lo, size)]
-        remote_copy(piece, piece, gather_send.at[k, n], gather_recv.at[k, n], **device).start()
-
-    def gather_arrived(k, size, n):
-        arrived(cols.at[k, 0, pl.ds(0, size)], gather_recv.at[k, n])
-
-    def e4(k):
-        arrived(pair.at[k], pair_recv.at[k])
-        cols[k, mp] = (grad_rings[k][3](yl) + pair[k].astype(F32)).astype(BF16)
-        gather_copy(k, mp, 0, rows, 0, **h_peer)
-        gather_copy(k, mp, 0, rows, 1, **x_next)
-        gather_copy(k, mp, 0, rows, 2, **x_prev)
-
-    def e5(k):
-        gather_arrived(k, rows, 0)
-        gather_copy(k, x * 2 + 1 - yh, 0, rows, 3, **x_next)
-        gather_copy(k, x * 2 + 1 - yh, 0, rows, 4, **x_prev)
-        gather_arrived(k, rows, 1)
-        gather_copy(k, xp * 2 + yh, 0, half, 5, **x_next)
-        gather_arrived(k, rows, 2)
-        gather_copy(k, xn * 2 + yh, half, half, 6, **x_prev)
-
-    def e6(k):
-        gather_arrived(k, rows, 3)
-        gather_copy(k, xp * 2 + 1 - yh, 0, half, 7, **x_next)
-        gather_arrived(k, rows, 4)
-        gather_copy(k, xn * 2 + 1 - yh, half, half, 8, **x_prev)
+        mine[j] = grad_rings[i].total(1 - yl).astype(BF16)
+        remote_copy(
+            mine.at[j], pair_piece(i), pair_send.at[i], pair_recv.at[i], **y_peer
+        ).start()
+
+    def gather_piece(i, m, which=None):
+        k, lo, size = places[i]
+        if which is not None:
+            size //= 2
+            lo += which * size
+        return cols.at[k, m, pl.ds(lo, size)]
+
+    def gather_copy(i, m, n, which=None, **device):
+        part = gather_piece(i, m, which)
+        remote_copy(part, part, gather_send.at[i, n], gather_recv.at[i, n], **device).start()
+
+    def gather_arrived(i, n):
+        arrived(gather_piece(i, 0, None if n < 5 else 0), gather_recv.at[i, n])
+
+    def e4(i):
+        k, lo, size = places[i]
+        arrived(pair_piece(i), pair_recv.at[i])
+        cols[k, mp, pl.ds(lo, size)] = (
+            grad_rings[i].total(yl) + pair_piece(i)[...].astype(F32)
+        ).astype(BF16)
+        gather_copy(i, mp, 0, **h_peer)
+        gather_copy(i, mp, 1, **x_next)
+        gather_copy(i, mp, 2, **x_prev)
+
+    def e5b(i):
+        gather_arrived(i, 0)
+        gather_copy(i, x * 2 + 1 - yh, 3, **x_next)
+        gather_copy(i, x * 2 + 1 - yh, 4, **x_prev)
+
+    def e5(i):
+        gather_arrived(i, 1)
+        gather_copy(i, xp * 2 + yh, 5, 0, **x_next)
+        gather_arrived(i, 2)
+        gather_copy(i, xn * 2 + yh, 6, 1, **x_prev)
+
+    def e6(i):
+        gather_arrived(i, 3)
+        gather_copy(i, xp * 2 + 1 - yh, 7, 0, **x_next)
+        gather_arrived(i, 4)
+        gather_copy(i, xn * 2 + 1 - yh, 8, 1, **x_prev)
 
     def e7(k):
-        for n in (5, 6, 7, 8):
-            gather_arrived(k, half, n)
+        for i, place in enumerate(places):
+            if place[0] == k:
+                for n in (5, 6, 7, 8):
+                    gather_arrived(i, n)
         rotated = jnp.dot(
             panel_t[...], cols[k].reshape(8 * rows, width), preferred_element_type=F32
         ).astype(BF16)
@@ -276,21 +370,14 @@
             )
             turned[:, at] = term if k == 0 else turned[:, at] + term
 
-    stages = (e1, e2, e3, e4, e5, e6, e7)
-    for s in range(chunks + len(stages) - 1):
-        for i, stage in enumerate(stages):
-            if 0 <= s - i < chunks:
-                stage(s - i)
-        if s == 0:
-            panel_forward()
-        if s == 1:
-            panel_share()
-        if s == 2:
-            panel_turn()
-        if s == 3:
-            panel_share_h()
-        if s == 4:
-            panel_join()
+    run(
+        order[0],
+        e1=e1, e1b=e1b, e1c=e1c, e2=e2, e3=e3, e4=e4, e5=e5, e5b=e5b, e6=e6, e7=e7,
+        panel_f1=lambda _: panel_forward(), panel_f2=lambda _: panel_forward_far(),
+        panel_share=lambda _: panel_share(), panel_turn=lambda _: panel_turn(),
+        panel_h=panel_h_copy, panel_share_h=lambda _: panel_share_h(),
+        panel_join=lambda _: panel_join(),
+    )
 
     arrived(moment, load_sem.at[2])
     arrived(square, load_sem.at[3])
@@ -315,13 +402,14 @@
             scaled[...], basis[at], (((1,), (1,)), ((), ())), preferred_element_type=F32
         ).astype(BF16)
 
-    for k in range(parts):
+    def back_send_part(k):
         back_out[k] = back_part(1 - yh, k)
         remote_copy(
             back_out.at[k], back.at[k, pl.ds(rows, rows)], back_send.at[k], back_recv.at[k],
             **h_peer,
         ).start()
-    for k in range(parts):
+
+    def back_keep_part(k):
         back[k, pl.ds(0, rows)] = back_part(yh, k)
 
     def outer_terms(j, carry):
@@ -334,13 +422,15 @@
         outer[1, j] = total[half:].astype(BF16)
         return carry
 
-    def outer_start():
-        lax.fori_loop(0, 8, outer_terms, 0)
+    def outer_part(i):
+        lax.fori_loop(i * 2, i * 2 + 2, outer_terms, 0)
+
+    def outer_share():
         remote_copy(
             outer.at[1 - c], outer_swap, outer_send.at[6], outer_recv.at[6], **core_peer
         ).start()
 
-    outer_ring_stages = ring_stages(
+    outer_rings = ring_stages(
         outer.at[c], outer_ring, outer_send, outer_recv, z, zn, zp, zo, z_next, z_prev
     )
 
@@ -350,15 +440,17 @@
         def add(j):
             outer[c, j] = (outer[c, j].astype(F32) + outer_swap[j].astype(F32)).astype(BF16)
 
-        outer_ring_stages[0](add)
+        outer_rings.far(add)
+        outer_rings.near(add)
+        outer_rings.rest(add)
 
     def l2():
-        outer_ring_stages[1]()
+        outer_rings.second()
 
     def l3():
-        outer_ring_stages[2]()
+        outer_rings.third()
         j = z * 2 + 1 - yl
-        outer[c, j] = outer_ring_stages[3](1 - yl).astype(BF16)
+        outer[c, j] = outer_rings.total(1 - yl).astype(BF16)
         remote_copy(
             outer.at[c, j], outer_pair, outer_send.at[7], outer_recv.at[7], **y_peer
         ).start()
@@ -366,7 +458,7 @@
     def l4():
         arrived(outer_pair, outer_recv.at[7])
         arrived(lstats, load_sem.at[4])
-        total = outer_ring_stages[3](yl) + outer_pair[...].astype(F32)
+        total = outer_rings.total(yl) + outer_pair[...].astype(F32)
         lstats[...] = beta_stats * lstats[...] + (1.0 - beta_stats) * total
         local_copy(lstats, left_out, out_sem.at[2]).start()
 
@@ -394,26 +486,34 @@
         for k in range(parts)
     ]
 
-    def u1(k):
-        arrived(back.at[k, pl.ds(0, rows)], back_recv.at[k])
-
+    def u1_term(k):
         def term(j):
             terms[k, j] = jnp.dot(
                 panel_cat[j], back[k], preferred_element_type=F32
             ).astype(BF16)
 
-        term_rings[k][0](term)
+        return term
+
+    def u1(k):
+        arrived(back.at[k, pl.ds(0, rows)], back_recv.at[k])
+        term_rings[k].far(u1_term(k))
+
+    def u1b(k):
+        term_rings[k].near(u1_term(k))
+
+    def u1c(k):
+        term_rings[k].rest(u1_term(k))
 
     def u2(k):
-        term_rings[k][1]()
+        term_rings[k].second()
 
     def u3(k):
-        term_rings[k][2]()
-        halves_out[k] = term_rings[k][3](1 - yh).astype(BF16)
+        term_rings[k].third()
+        halves_out[k] = term_rings[k].total(1 - yh).astype(BF16)
         remote_copy(
             halves_out.at[k], halves.at[yh, k], halves_send.at[k], halves_recv.at[k], **h_peer
         ).start()
-        halves[yh, k] = term_rings[k][3](yh).astype(BF16)
+        halves[yh, k] = term_rings[k].total(yh).astype(BF16)
         local_copy(
             halves.at[yh, k],
             update_out.at[:, pl.ds(pl.multiple_of(yh * hold + k * part, 128), part)],
@@ -428,30 +528,33 @@
             out_sem.at[5],
         ).start()
 
-    extras = {0: (outer_start,), 1: (l1,), 2: (l2, right_terms), 3: (l3,), 4: (l4,)}
-    late = (u1, u2, u3, u4)
-    for s in range(max(parts + len(late) - 1, 5)):
-        for i, stage in enumerate(late):
-            if 0 <= s - i < parts:
-                stage(s - i)
-        for extra in extras.get(s, ()):
-            extra()
-
-    for n in range(7):
+    run(
+        order[1],
+        bo=back_send_part, bi=back_keep_part, u1=u1, u1b=u1b, u1c=u1c, u2=u2, u3=u3, u4=u4,
+        outer=outer_part, outer_send=lambda _: outer_share(),
+        l1=lambda _: l1(), l2=lambda _: l2(), l3=lambda _: l3(), l4=lambda _: l4(),
+        right=lambda _: right_terms(),
+    )
+
+    for n in (0, 1, 2, 5, 6, 17):
         arrived(panel.at[0, 0], panel_send.at[n])
-    for n in range(7, 10):
+    for n in (3, 4):
+        arrived(panel.at[0, 0, pl.ds(0, depth // 2)], panel_send.at[n])
+    for n in range(7, 9):
         arrived(panel.at[0], panel_send.at[n])
-    for k in range(chunks):
-        arrived(swap.at[k], swap_send.at[k])
-        grad_rings[k][4]()
-        arrived(pair.at[k], pair_send.at[k])
+    for n in range(9, 17):
+        arrived(panel.at[0, 0], panel_send.at[n])
+    for i in range(len(places)):
+        arrived(piece(swap, i), swap_send.at[i])
+        grad_rings[i].sent()
+        arrived(pair_piece(i), pair_send.at[i])
         for n in range(9):
-            arrived(cols.at[k, 0, pl.ds(0, rows if n < 5 else half)], gather_send.at[k, n])
+            arrived(gather_piece(i, 0, None if n < 5 else 0), gather_send.at[i, n])
     for k in range(parts):
         arrived(back_out.at[k], back_send.at[k])
-        term_rings[k][4]()
+        term_rings[k].sent()
         arrived(halves_out.at[k], halves_send.at[k])
-    outer_ring_stages[4]()
+    outer_rings.sent()
     arrived(outer_swap, outer_send.at[6])
     arrived(outer_pair, outer_send.at[7])
     arrived(moment, out_sem.at[0])
@@ -462,9 +565,28 @@
     arrived(halves.at[0], out_sem.at[5])
 
 
+def hand_over(*refs):
+    ins, outs, buffers, in_sems, out_sems = refs[:5], refs[5:10], refs[10:15], refs[15], refs[16]
+    cuts = 4
+    pieces = []
+    for i in range(5):
+        count = cuts if i < 3 else 1
+        size = ins[i].shape[0] // count
+        for n in range(count):
+            at = pl.ds(n * size, size)
+            pieces.append((i, n, at))
+    for i, n, at in pieces:
+        local_copy(ins[i].at[at], buffers[i].at[at], in_sems.at[i, n]).start()
+    for i, n, at in pieces:
+        arrived(buffers[i].at[at], in_sems.at[i, n])
+        local_copy(buffers[i].at[at], outs[i].at[at], out_sems.at[i, n]).start()
+    for i, n, at in pieces:
+        arrived(buffers[i].at[at], out_sems.at[i, n])
+
+
 def on_device(
     gradients, left_basis, right_basis, first_moment, second_moment, left_stats, right_stats,
-    chunks=4, parts=4,
+    chunks=8, parts=4, places=PLACES, order=ORDER,
 ):
     rows, block = gradients.shape[1], gradients.shape[2] // 16
     width = block // chunks
@@ -477,8 +599,8 @@
     def buffer(*shape, dtype=BF16):
         return pltpu.VMEM(shape, dtype)
 
-    return pl.pallas_call(
-        functools.partial(step_kernel, chunks, parts),
+    results = pl.pallas_call(
+        functools.partial(step_kernel, places, parts, order),
         name="soap_step",
         out_shape=(
             jax.ShapeDtypeStruct((rows, block), BF16),
@@ -518,17 +640,17 @@
             buffer(share, block, dtype=F32),
             buffer(share, 8 * rows),
             dma((6,)),
-            dma((chunks,)),
-            dma((chunks,)),
-            dma((chunks,)),
-            dma((chunks, 6)),
-            dma((chunks, 6)),
-            dma((chunks,)),
-            dma((chunks,)),
-            dma((chunks, 9)),
-            dma((chunks, 9)),
-            dma((10,)),
-            dma((10,)),
+            dma((len(places),)),
+            dma((len(places),)),
+            dma((len(places),)),
+            dma((len(places), 6)),
+            dma((len(places), 6)),
+            dma((len(places),)),
+            dma((len(places),)),
+            dma((len(places), 9)),
+            dma((len(places), 9)),
+            dma((18,)),
+            dma((18,)),
             dma((parts,)),
             dma((parts,)),
             dma((parts, 6)),
@@ -543,6 +665,14 @@
             collective_id=0, has_side_effects=True, vmem_limit_bytes=62 * 1024 * 1024
         ),
     )(gradients, left_basis, right_basis, first_moment, second_moment, left_stats, right_stats)
+    return pl.pallas_call(
+        hand_over,
+        name="hand_over",
+        out_shape=tuple(jax.ShapeDtypeStruct(r.shape, r.dtype) for r in results),
+        in_specs=[any_space] * 5,
+        out_specs=(any_space,) * 5,
+        scratch_shapes=[pltpu.VMEM(r.shape, r.dtype) for r in results] + [dma((5, 4)), dma((5, 4))],
+    )(*results)
 
 
 def solution(mesh):

time: 146 us -> 123 us (0.84)
  Pallas kernels: 139 us -> 122 us
  local copies, waits for them, and re-layouts: 6.53 us -> 0 us
    pallas_call x1 -> x2, Pallas kernels: 139 us -> 122 us  [the longest x1 118 us: on_device(): pl.pallas_call(functools.partial(step_kernel, places, parts, order), name...]
    unnamed x13 -> x0, local copies, waits for them, and re-layouts: 6.53 us -> none
where the time goes in v3:
time: 123 us
  Pallas kernels  122 us (99%)
    pallas_call x1, Pallas kernels, on_device(): pl.pallas_call(functools.partial(step_kernel, places, parts, order), name...  118 us
    pallas_call x1, Pallas kernels, on_device(): pl.pallas_call(hand_over, name='hand_over', out_shape=tuple((jax.ShapeDty...  4.26 us

profile of v3, /device:TPU:0, one launch (start us, length us, event | category | flops | bytes accessed | tf_op | source)
XLA Modules:
  0.0 122.8 jit_solution(17957438596373194433)
XLA Ops:
  0.6 117.7 %soap_step.1 = (bf16[320,1024]{1,0:T(8,128)(2,1)}, f32[320,1024]{1,0:T(8,128)}, f32[320,1024]{1,0:T(8,128)}, f32[160,320]{1,0:T(8,128)}, f32[1,128,1024]{2,1,0:T(8,128)}) custom-call(bf16[1,320,16384]{2,1,0:T(8,128)(2,1)} %grads.1, bf16[160,320]{1,0:T(8,128)(2,1)} %left.1, bf16[1,1024,1024]{2,1,0:T(8,128)(2,1)} %right.1, f32[320,1024]{1,0:T(8,128)} %first.1, ...), custom_call_target="tpu_custom_call" | custom-call | tf_op jit(solution)/shard_map/soap_step/pallas_call | solution.py:602
  118.3 4.3 %hand_over.1 = (bf16[320,1024]{1,0:T(8,128)(2,1)}, f32[320,1024]{1,0:T(8,128)}, f32[320,1024]{1,0:T(8,128)}, f32[160,320]{1,0:T(8,128)}, f32[1,128,1024]{2,1,0:T(8,128)}) custom-call(bf16[320,1024]{1,0:T(8,128)(2,1)} %get-tuple-element.10.refs_0_, f32[320,1024]{1,0:T(8,128)} %get-tuple-element.11.refs_1_, f32[320,1024]{1,0:T(8,128)} %get-tuple-element.12.refs_2_, ...), custom_call_target="tpu_custom_call" | custom-call | tf_op jit(solution)/shard_map/hand_over/pallas_call | solution.py:668

commit v4 on v3

--- a/solution.py
+++ b/solution.py
@@ -61,11 +61,13 @@
     ),
     (
         ("bo", 0), ("bo", 1), ("bo", 2), ("bo", 3), ("bi", 0), ("bi", 1), ("bi", 2), ("bi", 3),
-        ("outer", 0), ("outer", 1), ("outer", 2), ("u1", 0), ("outer", 3), ("u1b", 0), ("u1c", 0),
-        ("outer_send", 0), ("right", 0), ("u1", 1), ("u2", 0), ("l1", 0), ("u1b", 1), ("u1c", 1),
-        ("u2", 1), ("u3", 0), ("u1", 2), ("l2", 0), ("u1b", 2), ("u1c", 2), ("u3", 1), ("u1", 3),
-        ("u4", 0), ("u2", 2), ("l3", 0), ("u1b", 3), ("u1c", 3), ("u4", 1), ("u2", 3), ("u3", 2),
-        ("l4", 0), ("u3", 3), ("u4", 2), ("u4", 3),
+        ("outer", 0), ("outer", 1), ("outer", 2), ("outer", 3), ("outer", 4), ("u1", 0),
+        ("outer", 5), ("u1b", 0), ("u1c", 0), ("outer", 6), ("u1", 1), ("outer", 7),
+        ("outer_send", 0), ("right", 0), ("right", 1), ("u1b", 1), ("u1c", 1), ("u2", 0),
+        ("right", 2), ("right", 3), ("right", 4), ("right", 5), ("right", 6), ("right", 7),
+        ("l1", 0), ("u1", 2), ("u2", 1), ("u1b", 2), ("u1c", 2), ("u3", 0), ("l2", 0), ("u1", 3),
+        ("u2", 2), ("u3", 1), ("u4", 0), ("u1b", 3), ("u1c", 3), ("l3", 0), ("u2", 3), ("u4", 1),
+        ("u3", 2), ("l4", 0), ("u3", 3), ("u4", 2), ("u4", 3),
     ),
 )
 
@@ -423,7 +425,7 @@
         return carry
 
     def outer_part(i):
-        lax.fori_loop(i * 2, i * 2 + 2, outer_terms, 0)
+        lax.fori_loop(i, i + 1, outer_terms, 0)
 
     def outer_share():
         remote_copy(
@@ -462,21 +464,20 @@
         lstats[...] = beta_stats * lstats[...] + (1.0 - beta_stats) * total
         local_copy(lstats, left_out, out_sem.at[2]).start()
 
-    def right_terms():
-        share = rstats.shape[0]
-        k_own = (mp * share) // width
-        off = pl.ds(pl.multiple_of((mp * share) % width, 128), share)
-        for i in range(4):
-            two = cols[k_own, pl.ds(2 * i, 2), :, off].reshape(2 * rows, share)
-            slice_t[:, pl.ds(i * 2 * rows, 2 * rows)] = two.T
-        arrived(rstats, load_sem.at[5])
-        for k in range(chunks):
-            at = pl.ds(k * width, width)
-            term = jnp.dot(
-                slice_t[...], cols[k].reshape(8 * rows, width), preferred_element_type=F32
-            )
-            rstats[:, at] = beta_stats * rstats[:, at] + (1.0 - beta_stats) * term
-        local_copy(rstats, right_out.at[0], out_sem.at[3]).start()
+    def right_terms(k):
+        if k == 0:
+            share = rstats.shape[0]
+            k_own = (mp * share) // width
+            off = pl.ds(pl.multiple_of((mp * share) % width, 128), share)
+            for i in range(4):
+                two = cols[k_own, pl.ds(2 * i, 2), :, off].reshape(2 * rows, share)
+                slice_t[:, pl.ds(i * 2 * rows, 2 * rows)] = two.T
+            arrived(rstats, load_sem.at[5])
+        at = pl.ds(k * width, width)
+        term = jnp.dot(slice_t[...], cols[k].reshape(8 * rows, width), preferred_element_type=F32)
+        rstats[:, at] = beta_stats * rstats[:, at] + (1.0 - beta_stats) * term
+        if k == chunks - 1:
+            local_copy(rstats, right_out.at[0], out_sem.at[3]).start()
 
     term_rings = [
         ring_stages(
@@ -533,7 +534,7 @@
         bo=back_send_part, bi=back_keep_part, u1=u1, u1b=u1b, u1c=u1c, u2=u2, u3=u3, u4=u4,
         outer=outer_part, outer_send=lambda _: outer_share(),
         l1=lambda _: l1(), l2=lambda _: l2(), l3=lambda _: l3(), l4=lambda _: l4(),
-        right=lambda _: right_terms(),
+        right=right_terms,
     )
 
     for n in (0, 1, 2, 5, 6, 17):

time: 123 us -> 121 us (0.984)
  Pallas kernels: 122 us -> 120 us
    pallas_call x1, Pallas kernels: 118 us -> 115 us  [on_device(): pl.pallas_call(functools.partial(step_kernel, places, parts, order), name...]
where the time goes in v4:
time: 121 us
  Pallas kernels  120 us (99%)
    pallas_call x1, Pallas kernels, on_device(): pl.pallas_call(functools.partial(step_kernel, places, parts, order), name...  115 us
    pallas_call x1, Pallas kernels, on_device(): pl.pallas_call(hand_over, name='hand_over', out_shape=tuple((jax.ShapeDty...  4.26 us

profile of v4, /device:TPU:0, one launch (start us, length us, event | category | flops | bytes accessed | tf_op | source)
XLA Modules:
  0.0 120.5 jit_solution(12449415950158894813)
XLA Ops:
  0.6 115.4 %soap_step.1 = (bf16[320,1024]{1,0:T(8,128)(2,1)}, f32[320,1024]{1,0:T(8,128)}, f32[320,1024]{1,0:T(8,128)}, f32[160,320]{1,0:T(8,128)}, f32[1,128,1024]{2,1,0:T(8,128)}) custom-call(bf16[1,320,16384]{2,1,0:T(8,128)(2,1)} %grads.1, bf16[160,320]{1,0:T(8,128)(2,1)} %left.1, bf16[1,1024,1024]{2,1,0:T(8,128)(2,1)} %right.1, f32[320,1024]{1,0:T(8,128)} %first.1, ...), custom_call_target="tpu_custom_call" | custom-call | tf_op jit(solution)/shard_map/soap_step/pallas_call | solution.py:603
  116.1 4.3 %hand_over.1 = (bf16[320,1024]{1,0:T(8,128)(2,1)}, f32[320,1024]{1,0:T(8,128)}, f32[320,1024]{1,0:T(8,128)}, f32[160,320]{1,0:T(8,128)}, f32[1,128,1024]{2,1,0:T(8,128)}) custom-call(bf16[320,1024]{1,0:T(8,128)(2,1)} %get-tuple-element.10.refs_0_, f32[320,1024]{1,0:T(8,128)} %get-tuple-element.11.refs_1_, f32[320,1024]{1,0:T(8,128)} %get-tuple-element.12.refs_2_, ...), custom_call_target="tpu_custom_call" | custom-call | tf_op jit(solution)/shard_map/hand_over/pallas_call | solution.py:669

commit v5 on v4

--- a/solution.py
+++ b/solution.py
@@ -56,8 +56,8 @@
         ("panel_h", 6), ("e6", 2), ("e4", 4), ("e2", 6), ("e1b", 7), ("e1c", 7), ("e4", 5),
         ("e6", 3), ("e2", 7), ("e7", 2), ("e3", 6), ("panel_h", 7), ("e5", 4), ("e5b", 4),
         ("e5", 5), ("e5b", 5), ("e7", 3), ("e3", 7), ("e4", 6), ("panel_share_h", 0), ("e6", 4),
-        ("e6", 5), ("e4", 7), ("panel_join", 0), ("e5", 6), ("e5b", 6), ("e7", 4), ("e7", 5),
-        ("e5b", 7), ("e5", 7), ("e6", 6), ("e6", 7), ("e7", 6), ("e7", 7),
+        ("e6", 5), ("e4", 7), ("e5", 6), ("e5b", 6), ("e7", 4), ("e7", 5),
+        ("e5b", 7), ("e5", 7), ("e6", 6), ("e6", 7), ("panel_join", 0), ("e7", 6), ("e7", 7),
     ),
     (
         ("bo", 0), ("bo", 1), ("bo", 2), ("bo", 3), ("bi", 0), ("bi", 1), ("bi", 2), ("bi", 3),

time: 121 us -> 121 us (level)
  no operation moved by 1% of the time
where the time goes in v5:
time: 121 us
  Pallas kernels  120 us (99%)
    pallas_call x1, Pallas kernels, on_device(): pl.pallas_call(functools.partial(step_kernel, places, parts, order), name...  115 us
    pallas_call x1, Pallas kernels, on_device(): pl.pallas_call(hand_over, name='hand_over', out_shape=tuple((jax.ShapeDty...  4.26 us

profile of v5, /device:TPU:0, one launch (start us, length us, event | category | flops | bytes accessed | tf_op | source)
XLA Modules:
  0.0 120.5 jit_solution(8032651674391873907)
XLA Ops:
  0.6 115.4 %soap_step.1 = (bf16[320,1024]{1,0:T(8,128)(2,1)}, f32[320,1024]{1,0:T(8,128)}, f32[320,1024]{1,0:T(8,128)}, f32[160,320]{1,0:T(8,128)}, f32[1,128,1024]{2,1,0:T(8,128)}) custom-call(bf16[1,320,16384]{2,1,0:T(8,128)(2,1)} %grads.1, bf16[160,320]{1,0:T(8,128)(2,1)} %left.1, bf16[1,1024,1024]{2,1,0:T(8,128)(2,1)} %right.1, f32[320,1024]{1,0:T(8,128)} %first.1, ...), custom_call_target="tpu_custom_call" | custom-call | tf_op jit(solution)/shard_map/soap_step/pallas_call | solution.py:603
  116.1 4.3 %hand_over.1 = (bf16[320,1024]{1,0:T(8,128)(2,1)}, f32[320,1024]{1,0:T(8,128)}, f32[320,1024]{1,0:T(8,128)}, f32[160,320]{1,0:T(8,128)}, f32[1,128,1024]{2,1,0:T(8,128)}) custom-call(bf16[320,1024]{1,0:T(8,128)(2,1)} %get-tuple-element.10.refs_0_, f32[320,1024]{1,0:T(8,128)} %get-tuple-element.11.refs_1_, f32[320,1024]{1,0:T(8,128)} %get-tuple-element.12.refs_2_, ...), custom_call_target="tpu_custom_call" | custom-call | tf_op jit(solution)/shard_map/hand_over/pallas_call | solution.py:669
